TPU v7x, 32 devices: a whole 2x2x4 slice. The times are simulated.
32 devices in a mesh: seq: 8 (over y, x, core), tensor: 4 (over z).
Axes of the slice: x: 2, y: 2, z: 4, core: 2. Of those that a mesh axis runs over, the one named last changes fastest.
Arguments:
- out_grad: bfloat16 [1024, 4096], P('seq', 'tensor'), may hold values from -3 to 3
- down_weight: bfloat16 [8, 256, 4096], P('tensor'), may hold values from -0.09375 to 0.09375
- pre_act: bfloat16 [8, 8, 128, 512], P('seq', 'tensor'), may hold values from -6 to 6
- gate_prob: float32 [8, 8, 128], P('seq', 'tensor'), may hold values from 0.1 to 1
- slot_token: int32 [8, 8, 128], P('seq', 'tensor'), may hold values from 0 to 127, as said below
- slot_count: int32 [8, 8], P('seq', 'tensor'), may hold values from 16 to 128, as said below
Outputs:
- pre_grad: bfloat16 [8, 8, 128, 512], P('seq', 'tensor')
- prob_grad: float32 [8, 8, 128], P('seq', 'tensor')
- weight_grad: bfloat16 [8, 256, 4096], P('tensor', None, 'seq')
Inputs may be any that keep to these rules, and one draw needn't show every extreme that they name: `slot_token`: for each group and expert the 128 slots list every token of the group once; slots from slot_count on hold tokens too and are not live. `slot_count`: some expert of some group has all 128 slots live.
All inputs are finite; a program needn't handle non-finite values.
Results may differ from a plain program's by a relative error of at most 0.015.
Values may be sent and summed in bfloat16 or wider, within the bound.
A program may use at most 64 MiB of HBM per device.

v0:
```python
import jax
import jax.numpy as jnp
from jax import lax
from jax.sharding import PartitionSpec as P


def expert_block(token_rows, pre_block, gate_probs, live_mask, expert_weight):
    width = expert_weight.shape[0]
    gate_val = pre_block[:, :width].astype(jnp.float32)
    up_val = pre_block[:, width:].astype(jnp.float32)
    sigma_gate = jax.nn.sigmoid(gate_val)
    silu_gate = gate_val * sigma_gate
    activation = (silu_gate * up_val).astype(jnp.bfloat16)
    raw_grad = lax.dot_general(
        token_rows, expert_weight, (((1,), (1,)), ((), ())), preferred_element_type=jnp.float32
    )
    prob_grad = jnp.where(
        live_mask, jnp.sum(activation.astype(jnp.float32) * raw_grad, axis=1), 0.0
    )
    hidden_grad = gate_probs[:, None] * raw_grad
    gate_grad = hidden_grad * up_val * sigma_gate * (1.0 + gate_val * (1.0 - sigma_gate))
    up_grad = hidden_grad * silu_gate
    pre_grad = jnp.where(
        live_mask[:, None], jnp.concatenate([gate_grad, up_grad], axis=1), 0.0
    ).astype(jnp.bfloat16)
    weighted = jnp.where(
        live_mask[:, None], gate_probs[:, None] * activation.astype(jnp.float32), 0.0
    ).astype(jnp.bfloat16)
    return (pre_grad, prob_grad, weighted)


def weight_part(weighted, token_rows):
    return lax.dot_general(
        weighted, token_rows, (((0,), (0,)), ((), ())), preferred_element_type=jnp.float32
    )


def per_device(out_grad, down_weight, pre_act, gate_prob, slot_token, slot_count):
    gathered = lax.all_gather(out_grad, "tensor", axis=1, tiled=True)
    expert_total = down_weight.shape[0]
    slot_total = slot_token.shape[2]
    positions = lax.broadcasted_iota(jnp.int32, (slot_total,), 0)
    pre_grads = []
    prob_grads = []
    weight_terms = []
    for expert in range(expert_total):
        expert_weight = down_weight[expert]
        live_count = slot_count[0, expert]
        token_rows = jnp.take(gathered, slot_token[0, expert], axis=0)
        live_mask = positions < live_count
        pre_block = pre_act[0, expert]
        gate_probs = gate_prob[0, expert]
        expert_pre, expert_prob, weighted = expert_block(
            token_rows, pre_block, gate_probs, live_mask, expert_weight
        )
        pre_grads.append(expert_pre)
        prob_grads.append(expert_prob)
        weight_terms.append(weight_part(weighted, token_rows))
    weight_grad = lax.psum_scatter(
        jnp.stack(weight_terms, axis=0).astype(jnp.bfloat16), "seq", scatter_dimension=2, tiled=True
    )
    pre_grad = jnp.stack(pre_grads, axis=0)[None]
    prob_grad = jnp.stack(prob_grads, axis=0)[None]
    return (pre_grad, prob_grad, weight_grad)


def solution(mesh):
    placed = (
        P("seq", "tensor"),
        P("tensor", None, None),
        P("seq", "tensor", None, None),
        P("seq", "tensor", None),
        P("seq", "tensor", None),
        P("seq", "tensor"),
    )
    return jax.shard_map(
        per_device,
        mesh=mesh,
        in_specs=placed,
        out_specs=(
            P("seq", "tensor", None, None),
            P("seq", "tensor", None),
            P("tensor", None, "seq"),
        ),
        check_vma=False,
    )
```

profile of v0, /device:TPU:0, one launch (start us, length us, event | category | flops | bytes accessed | tf_op | source)
XLA Modules:
  0.0 111.3 jit_solution(15295442529228637458)
XLA Ops:
  7.2 0.0 all-gather.2.cloned.1.call-start
  7.2 0.7 all-gather.2.cloned.1.call-update
  7.9 0.0 reduce-scatter.2.cloned.1.call-start
  7.9 1.3 %fusion.48 = (s32[1,1]{1,0:T(1,128)}, s32[1,1]{1,0:T(1,128)}) fusion(s32[1,2]{1,0:T(1,128)} %param.13), kind=kLoop, calls=%fused_computation.85 | loop fusion | bytes 16 | tf_op jit(solution)/shard_map/slice | solution.py:48
  9.3 0.6 iota_compare_fusion.1
  9.9 0.7 iota_compare_fusion
  10.6 0.8 compare_and_fusion.1
  11.4 0.8 slice_bitcast_fusion.3
  12.1 1.0 slice_bitcast_fusion.1
  13.1 27.1 %all-gather.2.cloned.1.call-done = bf16[128,4096]{1,0:T(8,128)(2,1)} async-done(((bf16[128,1024]{1,0:T(8,128)(2,1)}), bf16[128,4096]{1,0:T(8,128)(2,1)}) %all-gather.2.cloned.1.call-update) | async-done | bytes 1048592 | tf_op jit(solution)/shard_map/all_gather | solution.py:39
  40.2 0.0 copy-start
  40.2 4.6 %gather_fusion.1 = bf16[128,4096]{1,0:T(8,128)(2,1)} fusion(bf16[128,4096]{1,0:T(8,128)(2,1)} %all-gather.2.cloned.1.call-done, s32[1024]{0:T(1024)S(1)} %pad_clamp_fusion), kind=kCustom, calls=%fused_computation.1.clone | custom fusion | bytes 2097664 | tf_op jit(solution)/shard_map/jit(_take)/gather | solution.py:49
  44.9 2.0 %fusion.1 = bf16[1,256,4096]{2,1,0:T(8,128)(2,1)S(1)} fusion(bf16[128,4096]{1,0:T(8,128)(2,1)} %gather_fusion.1, pred[128]{0:T(512)(128)(4,1)S(1)} %get-tuple-element.16, f32[128]{0:T(128)S(1)} %get-tuple-element.15, pred[128]{0:T(512)(128)(4,1)S(1)} %iota_compare_fusion, bf16[128,512]{1,0:T(8,128)(2,1)S(1)} %get-tuple-element.13), kind=kOutput, calls=%fused_computation.5 | convolution fusion | flops 270401536 | bytes 3277568 | tf_op jit(solution)/shard_map/dot_general | solution.py:33
  46.9 0.0 copy-done
  46.9 2.2 %gather_fusion = bf16[128,4096]{1,0:T(8,128)(2,1)} fusion(bf16[128,4096]{1,0:T(8,128)(2,1)S(1)} %copy-done, s32[1024]{0:T(1024)S(1)} %pad_clamp_fusion.1), kind=kCustom, calls=%fused_computation.clone | custom fusion | bytes 2097664 | tf_op jit(solution)/shard_map/jit(_take)/gather | solution.py:49
  49.1 2.0 %fusion = bf16[1,256,4096]{2,1,0:T(8,128)(2,1)S(1)} fusion(bf16[128,4096]{1,0:T(8,128)(2,1)} %gather_fusion, pred[128]{0:T(512)(128)(4,1)S(1)} %get-tuple-element.4, f32[128]{0:T(128)S(1)} %get-tuple-element.14, pred[128]{0:T(512)(128)(4,1)S(1)} %iota_compare_fusion.1, bf16[128,512]{1,0:T(8,128)(2,1)S(1)} %get-tuple-element.12), kind=kOutput, calls=%fused_computation.4 | convolution fusion | flops 270401536 | bytes 3277568 | tf_op jit(solution)/shard_map/dot_general | solution.py:33
  51.1 2.3 %pad_maximum_fusion = bf16[2,256,4096]{2,1,0:T(8,128)(2,1)} fusion(bf16[1,256,4096]{2,1,0:T(8,128)(2,1)S(1)} %fusion.1, bf16[1,256,4096]{2,1,0:T(8,128)(2,1)S(1)} %fusion), kind=kLoop, calls=%fused_computation.6 | loop fusion | flops 2097152 | bytes 8388608 | tf_op jit(solution)/shard_map/stack | solution.py:60
  53.4 0.0 copy-start.2
  53.4 0.0 copy-start.1
  53.5 0.0 reduce-scatter.2.cloned.1.call-update
  53.5 1.2 %copy-done.2 = bf16[128,4096]{1,0:T(8,128)(2,1)S(1)} copy-done((bf16[128,4096]{1,0:T(8,128)(2,1)S(1)}, bf16[128,4096]{1,0:T(8,128)(2,1)}, u32[]{:S(2)}) %copy-start.2) | copy-done | bytes 1048600
  54.7 0.0 copy-start.3
  54.7 2.7 %fusion.18 = (f32[128]{0:T(128)S(1)}, f32[128,256]{1,0:T(8,128)S(1)}) fusion(bf16[128,512]{1,0:T(8,128)(2,1)S(1)} %get-tuple-element.12, bf16[2,256,4096]{2,1,0:T(8,128)(2,1)} %param.9, bf16[128,4096]{1,0:T(8,128)(2,1)S(1)} %copy-done.2, pred[128]{0:T(512)(128)(4,1)S(1)} %get-tuple-element.4), kind=kOutput, calls=%fused_computation.42 | convolution fusion | flops 269320064 | bytes 3408512 | tf_op jit(solution)/shard_map/dot_general | solution.py:14
  57.3 0.0 copy-done.1
  57.3 0.2 copy-done.3
  57.6 0.9 fusion.21
  58.5 1.3 %compare_select_fusion.2 = (f32[1,128]{1,0:T(1,128)S(1)}, f32[1,128]{1,0:T(1,128)S(1)}) fusion(f32[128]{0:T(128)S(1)} %get-tuple-element.20, s32[]{:T(128)} %bitcast.7, f32[128]{0:T(128)S(1)} %get-tuple-element.22, s32[]{:T(128)} %bitcast), kind=kLoop, calls=%fused_computation.72 | loop fusion | flops 512 | bytes 2056 | tf_op jit(solution)/shard_map/jit(_where)/select_n | solution.py:17
  59.8 0.6 maximum_bitcast_fusion.1
  60.4 0.2 fusion.12
  60.5 0.1 fusion.8
  60.6 0.1 fusion.9
  60.7 0.7 maximum_bitcast_fusion
  61.5 43.0 %reduce-scatter.2.cloned.1.call-done = bf16[2,256,512]{2,1,0:T(8,128)(2,1)} async-done(((bf16[2,256,4096]{2,1,0:T(8,128)(2,1)}), bf16[2,256,512]{2,1,0:T(8,128)(2,1)}) %reduce-scatter.2.cloned.1.call-update) | async-done | bytes 524304 | tf_op jit(solution)/shard_map/reduce_scatter | solution.py:59
  (2 shorter events, 0.0 us)
Async XLA Ops:
  7.2 33.1 %all-gather.2.cloned.1.call-start = ((), (), s32[]{:S(2)}) async-start(), calls=%async_computation.1 | async-start | bytes 1310720 | tf_op jit(solution)/shard_map/all_gather | solution.py:39
  7.9 96.5 %reduce-scatter.2.cloned.1.call-start = ((), (), s32[]{:S(2)}) async-start(), calls=%async_computation.2 | async-start | bytes 4718592 | tf_op jit(solution)/shard_map/reduce_scatter | solution.py:59
  40.2 6.7 %copy-start = (bf16[128,4096]{1,0:T(8,128)(2,1)S(1)}, bf16[128,4096]{1,0:T(8,128)(2,1)}, u32[]{:S(2)}) copy-start(bf16[128,4096]{1,0:T(8,128)(2,1)} %all-gather.2.cloned.1.call-done) | copy-start | bytes 3145732
  53.4 1.2 %copy-start.2 = (bf16[128,4096]{1,0:T(8,128)(2,1)S(1)}, bf16[128,4096]{1,0:T(8,128)(2,1)}, u32[]{:S(2)}) copy-start(bf16[128,4096]{1,0:T(8,128)(2,1)} %gather_fusion) | copy-start | bytes 3145732
  53.4 3.9 %copy-start.1 = (bf16[128,4096]{1,0:T(8,128)(2,1)S(1)}, bf16[128,4096]{1,0:T(8,128)(2,1)}, u32[]{:S(2)}) copy-start(bf16[128,4096]{1,0:T(8,128)(2,1)} %gather_fusion.1) | copy-start | bytes 3145732
  54.7 2.9 %copy-start.3 = (bf16[2,256,4096]{2,1,0:T(8,128)(2,1)S(1)}, bf16[2,256,4096]{2,1,0:T(8,128)(2,1)}, u32[]{:S(2)}) copy-start(bf16[2,256,4096]{2,1,0:T(8,128)(2,1)} %param.9) | copy-start | bytes 12582916
Sparse Core Ops, SparseCore 0:
  9.6 30.6 all-gather.1
  53.6 50.8 reduce-scatter.1
where the time goes:
time: 112 us; the launch traced here: 111 us
  waiting for transfers between devices  70.8 us (63%)
  between operations  14.1 us (13%)
  local copies, waits for them, and re-layouts  11.3 us (10%)
  matrix products  7.65 us (7%)
  other arithmetic  7.35 us (7%)
    reduce_scatter x1, waiting for transfers between devices, per_device(): lax.psum_scatter(jnp.stack(weight_terms, axis=0).astype(jnp.bfloat16), 's...  43 us
    all_gather x1, waiting for transfers between devices, per_device(): gathered = lax.all_gather(out_grad, 'tensor', axis=1, tiled=True)  27.1 us
    gather x2, local copies, waits for them, and re-layouts, per_device(): token_rows = jnp.take(gathered, slot_token[0, expert], axis=0)  6.81 us
    dot_general x2, matrix products, weight_part(): lax.dot_general(weighted, token_rows, (((0,), (0,)), ((), ())), preferred...  4.07 us
    dot_general x2, matrix products, expert_block(): lax.dot_general(token_rows, expert_weight, (((1,), (1,)), ((), ())), pref...  3.58 us
    another operation x1, other arithmetic, per_device(): jnp.stack(weight_terms, axis=0).astype(jnp.bfloat16)  2.31 us
  transfers between devices with their start and end apart: 2, of which 2 were waited for; matrix products, arithmetic and copies ran while one was open for 10% of the time, Pallas kernels for 0%

commit v1 on v0

v1 whole, which is shorter than its diff:
```python
import functools

import jax
import jax.numpy as jnp
from jax import lax
from jax.experimental import pallas as pl
from jax.experimental.pallas import tpu as pltpu
from jax.sharding import PartitionSpec as P

MESH = pl.DeviceIdType.MESH
PIECES = 2
AHEAD = 1


def token_slots(tok_ref, count_ref, expert, tokens):
    token = lax.broadcasted_iota(jnp.int32, (tokens, tokens), 0)
    slot = lax.broadcasted_iota(jnp.int32, (tokens, tokens), 1)
    hot = token == tok_ref[0, expert : expert + 1, :]
    return hot, hot & (slot < count_ref[0, expert])


def kernel(
    n_seq, n_tensor,
    count_ref, tok_ref, prob_ref, grad_ref, weight_ref, pre_ref,
    pre_out, prob_out, weight_out,
    rows, cols, scaled, weight, pre, coef, act, raw, total,
    local_sem, z_send, z_recv, c_send, c_recv, w_send, w_recv, f_send,
):
    s = lax.axis_index("seq")
    t = lax.axis_index("tensor")
    experts, hidden, _ = weight_ref.shape
    tokens = grad_ref.shape[0]
    block = cols.shape[1]
    halves = n_seq // n_tensor
    part = tokens // PIECES
    rounds = [(q, k) for q in range(PIECES) for k in range(halves)]
    sibling = s + 1 - 2 * lax.rem(s, 2)

    barrier = pltpu.get_barrier_semaphore()
    for i in range(1, n_seq):
        pl.semaphore_signal(barrier, inc=1, device_id=(lax.rem(s + i, n_seq), t), device_id_type=MESH)

    @pl.when(t > 0)
    def _():
        pl.semaphore_signal(barrier, inc=1, device_id=(s, t - 1), device_id_type=MESH)

    @pl.when(t < n_tensor - 1)
    def _():
        pl.semaphore_signal(barrier, inc=1, device_id=(s, t + 1), device_id_type=MESH)

    pre_copy = pltpu.make_async_copy(pre_ref.at[0], pre, local_sem.at[0])
    pre_copy.start()
    own_copies = []
    for k in range(halves):
        own_copies.append(
            pltpu.make_async_copy(
                grad_ref.at[:, pl.ds(k * block, block)], rows.at[t, k], local_sem.at[2 + k]
            )
        )
        own_copies[-1].start()
    weight_copy = pltpu.make_async_copy(weight_ref, weight, local_sem.at[1])
    weight_copy.start()
    pl.semaphore_wait(barrier, n_seq - 1 + (t > 0).astype(jnp.int32) + (t < n_tensor - 1).astype(jnp.int32))

    def piece(shard, q, k):
        return rows.at[shard, k, pl.ds(q * part, part), :]

    def source(shard, q, k, own):
        if own:
            return grad_ref.at[pl.ds(q * part, part), pl.ds(k * block, block)]
        return piece(shard, q, k)

    def z_copy(shard, q, k, way, own):
        p = q * halves + k
        return pltpu.make_async_remote_copy(
            src_ref=source(shard, q, k, own),
            dst_ref=piece(shard, q, k),
            send_sem=z_send.at[way, shard, p],
            recv_sem=z_recv.at[shard, p],
            device_id=(s, t + 1 if way == 0 else t - 1),
            device_id_type=MESH,
        )

    def c_copy(shard, q, k, own):
        return pltpu.make_async_remote_copy(
            src_ref=source(shard, q, k, own),
            dst_ref=cols.at[pl.ds(pl.multiple_of(s * tokens + q * part, part), part), :],
            send_sem=c_send.at[shard, q * halves + k],
            recv_sem=c_recv.at[s, q],
            device_id=(shard * halves + k, t),
            device_id_type=MESH,
        )

    def z_go(shard, q, k, way, own):
        @pl.when(t < n_tensor - 1 if way == 0 else t > 0)
        def _():
            z_copy(shard, q, k, way, own).start()

    def c_go(shard, q, k, own):
        @pl.when(shard * halves + k != s)
        def _():
            c_copy(shard, q, k, own).start()

    def w_copy(i):
        return pltpu.make_async_remote_copy(
            src_ref=scaled.at[pl.ds(pl.multiple_of(s * tokens, tokens), tokens), :],
            dst_ref=scaled.at[pl.ds(pl.multiple_of(s * tokens, tokens), tokens), :],
            send_sem=w_send.at[i],
            recv_sem=w_recv.at[s],
            device_id=(sibling if i == 0 else lax.rem(s + 2 * i, n_seq), t),
            device_id_type=MESH,
        )

    def f_copy(i):
        origin = lax.rem(s + n_seq - 2 * i, n_seq)
        at = scaled.at[pl.ds(pl.multiple_of(origin * tokens, tokens), tokens), :]
        return pltpu.make_async_remote_copy(
            src_ref=at, dst_ref=at, send_sem=f_send.at[i], recv_sem=w_recv.at[origin],
            device_id=(sibling, t), device_id_type=MESH,
        )

    def multiply(shard, q, k):
        left = rows[shard, k, q * part : (q + 1) * part, :]
        at = pl.ds(pl.multiple_of((shard * halves + k) * block, block), block)
        for e in range(experts):
            raw[q * part : (q + 1) * part, e * hidden : (e + 1) * hidden] += lax.dot_general(
                left, weight[e, :, at], (((1,), (1,)), ((), ())), preferred_element_type=jnp.float32
            )

    def send_own(p):
        q, k = rounds[p]
        z_go(t, q, k, 0, True)
        z_go(t, q, k, 1, True)
        c_go(t, q, k, True)

    for p in range(min(AHEAD + 1, len(rounds))):
        send_own(p)

    pre_copy.wait()
    for e in range(experts):
        hot, live = token_slots(tok_ref, count_ref, e, tokens)
        ordered = jnp.dot(hot.astype(jnp.bfloat16), pre[e], preferred_element_type=jnp.float32)
        probs = jnp.sum(jnp.where(live, prob_ref[0, e : e + 1, :], 0.0), axis=1, keepdims=True)
        gate, up = ordered[:, :hidden], ordered[:, hidden:]
        sigma = jax.nn.sigmoid(gate)
        silu = gate * sigma
        active = (silu * up).astype(jnp.bfloat16)
        act[:, e * hidden : (e + 1) * hidden] = active
        scaled[pl.ds(pl.multiple_of(s * tokens, tokens), tokens), e * hidden : (e + 1) * hidden] = (
            probs * active.astype(jnp.float32)
        ).astype(jnp.bfloat16)
        coef[e, :, :hidden] = probs * up * sigma * (1.0 + gate * (1.0 - sigma))
        coef[e, :, hidden:] = probs * silu
    for i in range(1, n_seq // 2):
        w_copy(i).start()
    w_copy(0).start()
    raw[...] = jnp.zeros_like(raw)
    for copy in own_copies:
        copy.wait()
    weight_copy.wait()

    def add_groups(q, first):
        for g in range(n_seq):
            at = pl.ds(g * tokens + q * part, part)
            term = lax.dot_general(
                scaled[at, :], cols[at, :], (((0,), (0,)), ((), ())), preferred_element_type=jnp.float32
            )
            if first and g == 0:
                total[...] = term
            else:
                total[...] += term

    def wait_groups(q):
        for g in range(n_seq):
            @pl.when(g != s)
            def _():
                at = cols.at[pl.ds(g * tokens + q * part, part), :]
                pltpu.make_async_remote_copy(
                    src_ref=at, dst_ref=at, send_sem=c_send.at[0, 0], recv_sem=c_recv.at[g, q],
                    device_id=(sibling, t), device_id_type=MESH,
                ).wait_recv()

    def use(shard, q, k):
        c_go(shard, q, k, False)
        multiply(shard, q, k)

    for p, (q, k) in enumerate(rounds):
        if p > 0 and p + AHEAD < len(rounds):
            send_own(p + AHEAD)
        for d in range(1, n_tensor):
            @pl.when(t >= d)
            def _():
                z_copy(t - d, q, k, 1, False).wait_recv()
                z_go(t - d, q, k, 0, False)
                use(t - d, q, k)

            @pl.when(t + d < n_tensor)
            def _():
                z_copy(t + d, q, k, 0, False).wait_recv()
                z_go(t + d, q, k, 1, False)
                use(t + d, q, k)
        multiply(t, q, k)
        if p == min(1, len(rounds) - 1):
            for i in range(1, n_seq // 2):
                f_copy(i).wait_recv()
                f_copy(i).start()

    cols[pl.ds(pl.multiple_of(s * tokens, tokens), tokens), :] = rows[lax.div(s, halves), lax.rem(s, halves)]
    for e in range(experts):
        hot, live = token_slots(tok_ref, count_ref, e, tokens)
        part_raw = raw[:, e * hidden : (e + 1) * hidden]
        grads = jnp.concatenate(
            [coef[e, :, :hidden] * part_raw, coef[e, :, hidden:] * part_raw], axis=1
        ).astype(jnp.bfloat16)
        pre_out[0, e] = lax.dot_general(
            hot.astype(jnp.bfloat16), grads, (((0,), (0,)), ((), ())), preferred_element_type=jnp.float32
        ).astype(jnp.bfloat16)
        sums = jnp.sum(
            act[:, e * hidden : (e + 1) * hidden].astype(jnp.float32) * part_raw, axis=1, keepdims=True
        )
        prob_out[0, e : e + 1, :] = jnp.sum(jnp.where(live, sums, 0.0), axis=0, keepdims=True)

    for g in range(n_seq):
        @pl.when(lax.rem(g, 2) != lax.rem(s, 2))
        def _():
            at = scaled.at[pl.ds(g * tokens, tokens), :]
            pltpu.make_async_remote_copy(
                src_ref=at, dst_ref=at, send_sem=w_send.at[0], recv_sem=w_recv.at[g],
                device_id=(sibling, t), device_id_type=MESH,
            ).wait_recv()
    for q in range(PIECES):
        wait_groups(q)
        add_groups(q, q == 0)
    for e in range(experts):
        weight_out[e] = total[e * hidden : (e + 1) * hidden, :].astype(jnp.bfloat16)

    for i in range(n_seq // 2):
        w_copy(i).wait_send()
    for i in range(1, n_seq // 2):
        f_copy(i).wait_send()
    for shard in range(n_tensor):
        for q, k in rounds:
            @pl.when(shard * halves + k != s)
            def _():
                c_copy(shard, q, k, False).wait_send()

            @pl.when((shard <= t) & (t < n_tensor - 1))
            def _():
                z_copy(shard, q, k, 0, False).wait_send()

            @pl.when((shard >= t) & (t > 0))
            def _():
                z_copy(shard, q, k, 1, False).wait_send()


def per_device(n_seq, n_tensor, out_grad, down_weight, pre_act, gate_prob, slot_token, slot_count):
    tokens, shard = out_grad.shape
    experts, hidden, width = down_weight.shape
    block = width // n_seq
    halves = n_seq // n_tensor
    pieces = PIECES * halves
    whole = pl.BlockSpec(memory_space=pltpu.VMEM)
    away = pl.BlockSpec(memory_space=pl.ANY)
    dma = pltpu.SemaphoreType.DMA
    return pl.pallas_call(
        functools.partial(kernel, n_seq, n_tensor),
        out_shape=(
            jax.ShapeDtypeStruct((1, experts, tokens, 2 * hidden), jnp.bfloat16),
            jax.ShapeDtypeStruct((1, experts, tokens), jnp.float32),
            jax.ShapeDtypeStruct((experts, hidden, block), jnp.bfloat16),
        ),
        in_specs=[pl.BlockSpec(memory_space=pltpu.SMEM), whole, whole, away, away, away],
        out_specs=(whole, whole, whole),
        scratch_shapes=[
            pltpu.VMEM((n_tensor, halves, tokens, block), jnp.bfloat16),
            pltpu.VMEM((n_seq * tokens, block), jnp.bfloat16),
            pltpu.VMEM((n_seq * tokens, experts * hidden), jnp.bfloat16),
            pltpu.VMEM((experts, hidden, width), jnp.bfloat16),
            pltpu.VMEM((experts, tokens, 2 * hidden), jnp.bfloat16),
            pltpu.VMEM((experts, tokens, 2 * hidden), jnp.float32),
            pltpu.VMEM((tokens, experts * hidden), jnp.bfloat16),
            pltpu.VMEM((tokens, experts * hidden), jnp.float32),
            pltpu.VMEM((experts * hidden, block), jnp.float32),
            dma((2 + halves,)),
            dma((2, n_tensor, pieces)),
            dma((n_tensor, pieces)),
            dma((n_tensor, pieces)),
            dma((n_seq, PIECES)),
            dma((n_seq // 2,)),
            dma((n_seq,)),
            dma((n_seq // 2,)),
        ],
        compiler_params=pltpu.CompilerParams(
            collective_id=0, has_side_effects=True, vmem_limit_bytes=40 * 1024 * 1024
        ),
    )(slot_count, slot_token, gate_prob, out_grad, down_weight, pre_act)


def solution(mesh):
    placed = (
        P("seq", "tensor"),
        P("tensor", None, None),
        P("seq", "tensor", None, None),
        P("seq", "tensor", None),
        P("seq", "tensor", None),
        P("seq", "tensor"),
    )
    return jax.shard_map(
        functools.partial(per_device, mesh.shape["seq"], mesh.shape["tensor"]),
        mesh=mesh,
        in_specs=placed,
        out_specs=(
            P("seq", "tensor", None, None),
            P("seq", "tensor", None),
            P("tensor", None, "seq"),
        ),
        check_vma=False,
    )
```

time: 112 us -> 45.7 us (0.41)
  the two profiles are of different devices: /device:TPU:0 before, /device:TPU:7 now
where the time goes in v1:
time: 45.7 us; the launch traced here: 45.1 us
  Pallas kernels  36.3 us (79%)
  local copies, waits for them, and re-layouts  8.15 us (18%)
  between operations  0.65 us (1%)
    pallas_call x1, Pallas kernels, per_device(): pl.pallas_call(functools.partial(kernel, n_seq, n_tensor), out_shape=(jax...  36.3 us
    unnamed x15, local copies, waits for them, and re-layouts  8.15 us

profile of v1, /device:TPU:7, one launch (start us, length us, event | category | flops | bytes accessed | tf_op | source)
XLA Modules:
  0.0 45.1 jit_solution(10951489270222418171)
XLA Ops:
  0.6 0.0 copy-start
  0.6 2.2 %copy-done = bf16[2,256,4096]{2,1,0:T(8,128)(2,1)S(1)} copy-done((bf16[2,256,4096]{2,1,0:T(8,128)(2,1)S(1)}, bf16[2,256,4096]{2,1,0:T(8,128)(2,1)}, u32[]{:S(2)}) %copy-start) | copy-done | bytes 4194328
  2.8 0.0 copy-start.1
  2.8 0.9 %copy-done.1 = bf16[128,1024]{1,0:T(8,128)(2,1)S(1)} copy-done((bf16[128,1024]{1,0:T(8,128)(2,1)S(1)}, bf16[128,1024]{1,0:T(8,128)(2,1)}, u32[]{:S(2)}) %copy-start.1) | copy-done | bytes 262168
  3.8 0.0 copy-start.2
  3.8 0.9 %copy-done.2 = bf16[1,2,128,512]{3,2,1,0:T(8,128)(2,1)S(1)} copy-done((bf16[1,2,128,512]{3,2,1,0:T(8,128)(2,1)S(1)}, bf16[1,2,128,512]{3,2,1,0:T(8,128)(2,1)}, u32[]{:S(2)}) %copy-start.2) | copy-done | bytes 262168
  4.7 0.0 copy-start.3
  4.7 0.7 %copy-done.3 = s32[1,2,128]{2,1,0:T(2,128)S(1)} copy-done((s32[1,2,128]{2,1,0:T(2,128)S(1)}, s32[1,2,128]{2,1,0:T(2,128)}, u32[]{:S(2)}) %copy-start.3) | copy-done | bytes 1048
  5.4 0.0 copy-start.4
  5.4 0.7 %copy-done.4 = f32[1,2,128]{2,1,0:T(2,128)S(1)} copy-done((f32[1,2,128]{2,1,0:T(2,128)S(1)}, f32[1,2,128]{2,1,0:T(2,128)}, u32[]{:S(2)}) %copy-start.4) | copy-done | bytes 1048
  6.1 0.0 copy-start.5
  6.1 0.7 %copy-done.5 = s32[1,2]{1,0:T(1,128)S(1)} copy-done((s32[1,2]{1,0:T(1,128)S(1)}, s32[1,2]{1,0:T(1,128)}, u32[]{:S(2)}) %copy-start.5) | copy-done | bytes 32
  6.7 36.3 %shard_map.85 = (bf16[1,2,128,512]{3,2,1,0:T(8,128)(2,1)S(1)}, f32[1,2,128]{2,1,0:T(2,128)S(1)}, bf16[2,256,512]{2,1,0:T(8,128)(2,1)S(1)}) custom-call(s32[1,2]{1,0:T(1,128)S(1)} %copy-done.5, s32[1,2,128]{2,1,0:T(2,128)S(1)} %copy-done.3, f32[1,2,128]{2,1,0:T(2,128)S(1)} %copy-done.4, bf16[128,1024]{1,0:T(8,128)(2,1)S(1)} %copy-done.1, ...), custom_call_target="tpu_custom_call" | custom-call | tf_op jit(solution)/shard_map/pallas_call | solution.py:265
  43.0 0.7 %copy.12 = bf16[1,2,128,512]{3,2,1,0:T(8,128)(2,1)} copy(bf16[1,2,128,512]{3,2,1,0:T(8,128)(2,1)S(1)} %get-tuple-element.6) | data formatting | bytes 524288
  43.7 0.6 %copy.13 = f32[1,2,128]{2,1,0:T(2,128)} copy(f32[1,2,128]{2,1,0:T(2,128)S(1)} %get-tuple-element.7) | data formatting | bytes 2048
  44.3 0.8 %copy.14 = bf16[2,256,512]{2,1,0:T(8,128)(2,1)} copy(bf16[2,256,512]{2,1,0:T(8,128)(2,1)S(1)} %get-tuple-element.8) | data formatting | bytes 1048576
Async XLA Ops:
  0.6 2.2 %copy-start = (bf16[2,256,4096]{2,1,0:T(8,128)(2,1)S(1)}, bf16[2,256,4096]{2,1,0:T(8,128)(2,1)}, u32[]{:S(2)}) copy-start(bf16[2,256,4096]{2,1,0:T(8,128)(2,1)} %weight_ref.1) | copy-start | bytes 12582916
  2.8 0.9 %copy-start.1 = (bf16[128,1024]{1,0:T(8,128)(2,1)S(1)}, bf16[128,1024]{1,0:T(8,128)(2,1)}, u32[]{:S(2)}) copy-start(bf16[128,1024]{1,0:T(8,128)(2,1)} %grad_ref.1) | copy-start | bytes 786436
  3.8 0.9 %copy-start.2 = (bf16[1,2,128,512]{3,2,1,0:T(8,128)(2,1)S(1)}, bf16[1,2,128,512]{3,2,1,0:T(8,128)(2,1)}, u32[]{:S(2)}) copy-start(bf16[1,2,128,512]{3,2,1,0:T(8,128)(2,1)} %pre_ref.1) | copy-start | bytes 786436
  4.7 0.7 %copy-start.3 = (s32[1,2,128]{2,1,0:T(2,128)S(1)}, s32[1,2,128]{2,1,0:T(2,128)}, u32[]{:S(2)}) copy-start(s32[1,2,128]{2,1,0:T(2,128)} %tok_ref.1) | copy-start | bytes 3076
  5.4 0.7 %copy-start.4 = (f32[1,2,128]{2,1,0:T(2,128)S(1)}, f32[1,2,128]{2,1,0:T(2,128)}, u32[]{:S(2)}) copy-start(f32[1,2,128]{2,1,0:T(2,128)} %prob_ref.1) | copy-start | bytes 3076
  6.1 0.7 %copy-start.5 = (s32[1,2]{1,0:T(1,128)S(1)}, s32[1,2]{1,0:T(1,128)}, u32[]{:S(2)}) copy-start(s32[1,2]{1,0:T(1,128)} %count_ref.1) | copy-start | bytes 28

commit v2 on v1

--- a/solution.py
+++ b/solution.py
@@ -10,21 +10,22 @@
 MESH = pl.DeviceIdType.MESH
 PIECES = 2
 AHEAD = 1
+DIRECT = 2
 
 
 def token_slots(tok_ref, count_ref, expert, tokens):
     token = lax.broadcasted_iota(jnp.int32, (tokens, tokens), 0)
     slot = lax.broadcasted_iota(jnp.int32, (tokens, tokens), 1)
-    hot = token == tok_ref[0, expert : expert + 1, :]
+    hot = token == tok_ref[expert : expert + 1, :]
     return hot, hot & (slot < count_ref[0, expert])
 
 
 def kernel(
     n_seq, n_tensor,
-    count_ref, tok_ref, prob_ref, grad_ref, weight_ref, pre_ref,
+    count_in, tok_in, prob_in, grad_ref, weight_ref, pre_ref,
     pre_out, prob_out, weight_out,
-    rows, cols, scaled, weight, pre, coef, act, raw, total,
-    local_sem, z_send, z_recv, c_send, c_recv, w_send, w_recv, f_send,
+    count_ref, tok_ref, prob_ref, rows, cols, scaled, weight, pre, coef, act, raw, total,
+    local_sem, o_send, z_send, z_recv, c_send, c_recv, w_send, w_recv, f_send,
 ):
     s = lax.axis_index("seq")
     t = lax.axis_index("tensor")
@@ -33,6 +34,7 @@
     block = cols.shape[1]
     halves = n_seq // n_tensor
     part = tokens // PIECES
+    reach = min(DIRECT, n_tensor - 1)
     rounds = [(q, k) for q in range(PIECES) for k in range(halves)]
     sibling = s + 1 - 2 * lax.rem(s, 2)
 
@@ -40,27 +42,37 @@
     for i in range(1, n_seq):
         pl.semaphore_signal(barrier, inc=1, device_id=(lax.rem(s + i, n_seq), t), device_id_type=MESH)
 
-    @pl.when(t > 0)
-    def _():
-        pl.semaphore_signal(barrier, inc=1, device_id=(s, t - 1), device_id_type=MESH)
-
-    @pl.when(t < n_tensor - 1)
-    def _():
-        pl.semaphore_signal(barrier, inc=1, device_id=(s, t + 1), device_id_type=MESH)
-
-    pre_copy = pltpu.make_async_copy(pre_ref.at[0], pre, local_sem.at[0])
-    pre_copy.start()
+    greeted = n_seq - 1
+    for steps in range(1, reach + 1):
+        @pl.when(t >= steps)
+        def _():
+            pl.semaphore_signal(barrier, inc=1, device_id=(s, t - steps), device_id_type=MESH)
+
+        @pl.when(t + steps < n_tensor)
+        def _():
+            pl.semaphore_signal(barrier, inc=1, device_id=(s, t + steps), device_id_type=MESH)
+
+        greeted += (t >= steps).astype(jnp.int32) + (t + steps < n_tensor).astype(jnp.int32)
+
+    first_copies = [
+        pltpu.make_async_copy(pre_ref.at[0], pre, local_sem.at[0]),
+        pltpu.make_async_copy(count_in, count_ref, local_sem.at[1]),
+        pltpu.make_async_copy(tok_in.at[0], tok_ref, local_sem.at[2]),
+        pltpu.make_async_copy(prob_in.at[0], prob_ref, local_sem.at[3]),
+    ]
+    for copy in first_copies:
+        copy.start()
     own_copies = []
     for k in range(halves):
         own_copies.append(
             pltpu.make_async_copy(
-                grad_ref.at[:, pl.ds(k * block, block)], rows.at[t, k], local_sem.at[2 + k]
+                grad_ref.at[:, pl.ds(k * block, block)], rows.at[t, k], local_sem.at[5 + k]
             )
         )
         own_copies[-1].start()
-    weight_copy = pltpu.make_async_copy(weight_ref, weight, local_sem.at[1])
+    weight_copy = pltpu.make_async_copy(weight_ref, weight, local_sem.at[4])
     weight_copy.start()
-    pl.semaphore_wait(barrier, n_seq - 1 + (t > 0).astype(jnp.int32) + (t < n_tensor - 1).astype(jnp.int32))
+    pl.semaphore_wait(barrier, greeted)
 
     def piece(shard, q, k):
         return rows.at[shard, k, pl.ds(q * part, part), :]
@@ -70,14 +82,14 @@
             return grad_ref.at[pl.ds(q * part, part), pl.ds(k * block, block)]
         return piece(shard, q, k)
 
-    def z_copy(shard, q, k, way, own):
+    def z_copy(shard, q, k, way, own, steps=1):
         p = q * halves + k
         return pltpu.make_async_remote_copy(
             src_ref=source(shard, q, k, own),
             dst_ref=piece(shard, q, k),
-            send_sem=z_send.at[way, shard, p],
+            send_sem=o_send.at[way, steps - 1, p] if own else z_send.at[way, shard, p],
             recv_sem=z_recv.at[shard, p],
-            device_id=(s, t + 1 if way == 0 else t - 1),
+            device_id=(s, t + steps if way == 0 else t - steps),
             device_id_type=MESH,
         )
 
@@ -91,10 +103,10 @@
             device_id_type=MESH,
         )
 
-    def z_go(shard, q, k, way, own):
-        @pl.when(t < n_tensor - 1 if way == 0 else t > 0)
-        def _():
-            z_copy(shard, q, k, way, own).start()
+    def z_go(shard, q, k, way, own, steps=1):
+        @pl.when(t + steps < n_tensor if way == 0 else t >= steps)
+        def _():
+            z_copy(shard, q, k, way, own, steps).start()
 
     def c_go(shard, q, k, own):
         @pl.when(shard * halves + k != s)
@@ -129,18 +141,20 @@
 
     def send_own(p):
         q, k = rounds[p]
-        z_go(t, q, k, 0, True)
-        z_go(t, q, k, 1, True)
+        for steps in range(reach, 0, -1):
+            z_go(t, q, k, 0, True, steps)
+            z_go(t, q, k, 1, True, steps)
         c_go(t, q, k, True)
 
     for p in range(min(AHEAD + 1, len(rounds))):
         send_own(p)
 
-    pre_copy.wait()
+    for copy in first_copies:
+        copy.wait()
     for e in range(experts):
         hot, live = token_slots(tok_ref, count_ref, e, tokens)
         ordered = jnp.dot(hot.astype(jnp.bfloat16), pre[e], preferred_element_type=jnp.float32)
-        probs = jnp.sum(jnp.where(live, prob_ref[0, e : e + 1, :], 0.0), axis=1, keepdims=True)
+        probs = jnp.sum(jnp.where(live, prob_ref[e : e + 1, :], 0.0), axis=1, keepdims=True)
         gate, up = ordered[:, :hidden], ordered[:, hidden:]
         sigma = jax.nn.sigmoid(gate)
         silu = gate * sigma
@@ -184,23 +198,32 @@
         c_go(shard, q, k, False)
         multiply(shard, q, k)
 
-    for p, (q, k) in enumerate(rounds):
-        if p > 0 and p + AHEAD < len(rounds):
-            send_own(p + AHEAD)
+    for tick in range(len(rounds) + n_tensor - 1 - reach):
+        if tick > 0 and tick + AHEAD < len(rounds):
+            send_own(tick + AHEAD)
         for d in range(1, n_tensor):
+            p = tick - max(0, d - reach)
+            if not 0 <= p < len(rounds):
+                continue
+            q, k = rounds[p]
+
             @pl.when(t >= d)
             def _():
                 z_copy(t - d, q, k, 1, False).wait_recv()
-                z_go(t - d, q, k, 0, False)
+                if d >= reach:
+                    z_go(t - d, q, k, 0, False)
                 use(t - d, q, k)
 
             @pl.when(t + d < n_tensor)
             def _():
                 z_copy(t + d, q, k, 0, False).wait_recv()
-                z_go(t + d, q, k, 1, False)
+                if d >= reach:
+                    z_go(t + d, q, k, 1, False)
                 use(t + d, q, k)
-        multiply(t, q, k)
-        if p == min(1, len(rounds) - 1):
+
+        if tick < len(rounds):
+            multiply(t, *rounds[tick])
+        if tick == min(1, len(rounds) - 1):
             for i in range(1, n_seq // 2):
                 f_copy(i).wait_recv()
                 f_copy(i).start()
@@ -244,13 +267,23 @@
             def _():
                 c_copy(shard, q, k, False).wait_send()
 
-            @pl.when((shard <= t) & (t < n_tensor - 1))
+            @pl.when((shard + reach <= t) & (t < n_tensor - 1))
             def _():
                 z_copy(shard, q, k, 0, False).wait_send()
 
-            @pl.when((shard >= t) & (t > 0))
+            @pl.when((shard - reach >= t) & (t > 0))
             def _():
                 z_copy(shard, q, k, 1, False).wait_send()
+
+    for q, k in rounds:
+        for steps in range(1, reach + 1):
+            @pl.when(t + steps < n_tensor)
+            def _():
+                z_copy(t, q, k, 0, True, steps).wait_send()
+
+            @pl.when(t >= steps)
+            def _():
+                z_copy(t, q, k, 1, True, steps).wait_send()
 
 
 def per_device(n_seq, n_tensor, out_grad, down_weight, pre_act, gate_prob, slot_token, slot_count):
@@ -259,8 +292,9 @@
     block = width // n_seq
     halves = n_seq // n_tensor
     pieces = PIECES * halves
+    reach = min(DIRECT, n_tensor - 1)
     whole = pl.BlockSpec(memory_space=pltpu.VMEM)
-    away = pl.BlockSpec(memory_space=pl.ANY)
+    away = pl.BlockSpec(memory_space=pltpu.HBM)
     dma = pltpu.SemaphoreType.DMA
     return pl.pallas_call(
         functools.partial(kernel, n_seq, n_tensor),
@@ -269,9 +303,12 @@
             jax.ShapeDtypeStruct((1, experts, tokens), jnp.float32),
             jax.ShapeDtypeStruct((experts, hidden, block), jnp.bfloat16),
         ),
-        in_specs=[pl.BlockSpec(memory_space=pltpu.SMEM), whole, whole, away, away, away],
+        in_specs=[away] * 6,
         out_specs=(whole, whole, whole),
         scratch_shapes=[
+            pltpu.SMEM((1, experts), jnp.int32),
+            pltpu.VMEM((experts, tokens), jnp.int32),
+            pltpu.VMEM((experts, tokens), jnp.float32),
             pltpu.VMEM((n_tensor, halves, tokens, block), jnp.bfloat16),
             pltpu.VMEM((n_seq * tokens, block), jnp.bfloat16),
             pltpu.VMEM((n_seq * tokens, experts * hidden), jnp.bfloat16),
@@ -281,7 +318,8 @@
             pltpu.VMEM((tokens, experts * hidden), jnp.bfloat16),
             pltpu.VMEM((tokens, experts * hidden), jnp.float32),
             pltpu.VMEM((experts * hidden, block), jnp.float32),
-            dma((2 + halves,)),
+            dma((5 + halves,)),
+            dma((2, reach, pieces)),
             dma((2, n_tensor, pieces)),
             dma((n_tensor, pieces)),
             dma((n_tensor, pieces)),
@@ -293,7 +331,12 @@
         compiler_params=pltpu.CompilerParams(
             collective_id=0, has_side_effects=True, vmem_limit_bytes=40 * 1024 * 1024
         ),
-    )(slot_count, slot_token, gate_prob, out_grad, down_weight, pre_act)
+    )(
+        *[
+            pltpu.with_memory_space_constraint(operand, pltpu.HBM)
+            for operand in (slot_count, slot_token, gate_prob, out_grad, down_weight, pre_act)
+        ]
+    )
 
 
 def solution(mesh):

time: 45.7 us -> 35.8 us (0.78)
  local copies, waits for them, and re-layouts: 8.15 us -> 2.06 us
  Pallas kernels: 36.3 us -> 32.4 us
    unnamed x15 -> x3, local copies, waits for them, and re-layouts: 8.15 us -> 2.06 us
    pallas_call x1, Pallas kernels: 36.3 us -> 32.4 us  [per_device(): pl.pallas_call(functools.partial(kernel, n_seq, n_tensor), out_shape=(jax...]
where the time goes in v2:
time: 35.8 us; the launch traced here: 35.1 us
  Pallas kernels  32.4 us (91%)
  local copies, waits for them, and re-layouts  2.06 us (6%)
  between operations  0.64 us (2%)
    pallas_call x1, Pallas kernels, per_device(): pl.pallas_call(functools.partial(kernel, n_seq, n_tensor), out_shape=(jax...  32.4 us
    unnamed x3, local copies, waits for them, and re-layouts  2.06 us

profile of v2, /device:TPU:7, one launch (start us, length us, event | category | flops | bytes accessed | tf_op | source)
XLA Modules:
  0.0 35.1 jit_solution(3624788916648642590)
XLA Ops:
  0.6 32.4 %shard_map.85 = (bf16[1,2,128,512]{3,2,1,0:T(8,128)(2,1)S(1)}, f32[1,2,128]{2,1,0:T(2,128)S(1)}, bf16[2,256,512]{2,1,0:T(8,128)(2,1)S(1)}) custom-call(s32[1,2]{1,0:T(1,128)} %count_in.1, s32[1,2,128]{2,1,0:T(2,128)} %tok_in.1, f32[1,2,128]{2,1,0:T(2,128)} %prob_in.1, bf16[128,1024]{1,0:T(8,128)(2,1)} %grad_ref.1, bf16[2,256,4096]{2,1,0:T(8,128)(2,1)} %weight_ref.1, ...), custom_call_target="tpu_custom_call" | custom-call | tf_op jit(solution)/shard_map/pallas_call | solution.py:299
  33.1 0.7 %copy.12 = bf16[1,2,128,512]{3,2,1,0:T(8,128)(2,1)} copy(bf16[1,2,128,512]{3,2,1,0:T(8,128)(2,1)S(1)} %get-tuple-element.6) | data formatting | bytes 524288
  33.8 0.6 %copy.13 = f32[1,2,128]{2,1,0:T(2,128)} copy(f32[1,2,128]{2,1,0:T(2,128)S(1)} %get-tuple-element.7) | data formatting | bytes 2048
  34.4 0.8 %copy.14 = bf16[2,256,512]{2,1,0:T(8,128)(2,1)} copy(bf16[2,256,512]{2,1,0:T(8,128)(2,1)S(1)} %get-tuple-element.8) | data formatting | bytes 1048576

commit v3 on v2

--- a/solution.py
+++ b/solution.py
@@ -10,7 +10,8 @@
 MESH = pl.DeviceIdType.MESH
 PIECES = 2
 AHEAD = 1
-DIRECT = 2
+EARLY = 2
+DIRECT = 1
 
 
 def token_slots(tok_ref, count_ref, expert, tokens):
@@ -31,7 +32,7 @@
     t = lax.axis_index("tensor")
     experts, hidden, _ = weight_ref.shape
     tokens = grad_ref.shape[0]
-    block = cols.shape[1]
+    block = cols.shape[2]
     halves = n_seq // n_tensor
     part = tokens // PIECES
     reach = min(DIRECT, n_tensor - 1)
@@ -96,7 +97,7 @@
     def c_copy(shard, q, k, own):
         return pltpu.make_async_remote_copy(
             src_ref=source(shard, q, k, own),
-            dst_ref=cols.at[pl.ds(pl.multiple_of(s * tokens + q * part, part), part), :],
+            dst_ref=cols.at[q, pl.ds(pl.multiple_of(s * part, part), part), :],
             send_sem=c_send.at[shard, q * halves + k],
             recv_sem=c_recv.at[s, q],
             device_id=(shard * halves + k, t),
@@ -113,10 +114,13 @@
         def _():
             c_copy(shard, q, k, own).start()
 
+    def group(origin):
+        return scaled.at[:, pl.ds(pl.multiple_of(origin * part, part), part), :]
+
     def w_copy(i):
         return pltpu.make_async_remote_copy(
-            src_ref=scaled.at[pl.ds(pl.multiple_of(s * tokens, tokens), tokens), :],
-            dst_ref=scaled.at[pl.ds(pl.multiple_of(s * tokens, tokens), tokens), :],
+            src_ref=group(s),
+            dst_ref=group(s),
             send_sem=w_send.at[i],
             recv_sem=w_recv.at[s],
             device_id=(sibling if i == 0 else lax.rem(s + 2 * i, n_seq), t),
@@ -125,7 +129,7 @@
 
     def f_copy(i):
         origin = lax.rem(s + n_seq - 2 * i, n_seq)
-        at = scaled.at[pl.ds(pl.multiple_of(origin * tokens, tokens), tokens), :]
+        at = group(origin)
         return pltpu.make_async_remote_copy(
             src_ref=at, dst_ref=at, send_sem=f_send.at[i], recv_sem=w_recv.at[origin],
             device_id=(sibling, t), device_id_type=MESH,
@@ -149,9 +153,7 @@
     for p in range(min(AHEAD + 1, len(rounds))):
         send_own(p)
 
-    for copy in first_copies:
-        copy.wait()
-    for e in range(experts):
+    def prepare(e):
         hot, live = token_slots(tok_ref, count_ref, e, tokens)
         ordered = jnp.dot(hot.astype(jnp.bfloat16), pre[e], preferred_element_type=jnp.float32)
         probs = jnp.sum(jnp.where(live, prob_ref[e : e + 1, :], 0.0), axis=1, keepdims=True)
@@ -160,75 +162,113 @@
         silu = gate * sigma
         active = (silu * up).astype(jnp.bfloat16)
         act[:, e * hidden : (e + 1) * hidden] = active
-        scaled[pl.ds(pl.multiple_of(s * tokens, tokens), tokens), e * hidden : (e + 1) * hidden] = (
-            probs * active.astype(jnp.float32)
-        ).astype(jnp.bfloat16)
+        weighted = (probs * active.astype(jnp.float32)).astype(jnp.bfloat16)
+        for q in range(PIECES):
+            scaled[
+                q, pl.ds(pl.multiple_of(s * part, part), part), e * hidden : (e + 1) * hidden
+            ] = weighted[q * part : (q + 1) * part]
         coef[e, :, :hidden] = probs * up * sigma * (1.0 + gate * (1.0 - sigma))
         coef[e, :, hidden:] = probs * silu
-    for i in range(1, n_seq // 2):
-        w_copy(i).start()
-    w_copy(0).start()
-    raw[...] = jnp.zeros_like(raw)
-    for copy in own_copies:
-        copy.wait()
-    weight_copy.wait()
-
-    def add_groups(q, first):
+
+    def add_groups(q):
+        for e in range(experts):
+            term = lax.dot_general(
+                scaled[q, :, e * hidden : (e + 1) * hidden], cols[q],
+                (((0,), (0,)), ((), ())), preferred_element_type=jnp.float32,
+            )
+            if q > 0:
+                term += total[e]
+            if q < PIECES - 1:
+                total[e] = term
+            else:
+                weight_out[e] = term.astype(jnp.bfloat16)
+
+    def wait_weighted():
         for g in range(n_seq):
-            at = pl.ds(g * tokens + q * part, part)
-            term = lax.dot_general(
-                scaled[at, :], cols[at, :], (((0,), (0,)), ((), ())), preferred_element_type=jnp.float32
-            )
-            if first and g == 0:
-                total[...] = term
-            else:
-                total[...] += term
+            @pl.when(lax.rem(g, 2) != lax.rem(s, 2))
+            def _():
+                at = group(g)
+                pltpu.make_async_remote_copy(
+                    src_ref=at, dst_ref=at, send_sem=w_send.at[0], recv_sem=w_recv.at[g],
+                    device_id=(sibling, t), device_id_type=MESH,
+                ).wait_recv()
 
     def wait_groups(q):
         for g in range(n_seq):
             @pl.when(g != s)
             def _():
-                at = cols.at[pl.ds(g * tokens + q * part, part), :]
+                at = cols.at[q, pl.ds(g * part, part), :]
                 pltpu.make_async_remote_copy(
                     src_ref=at, dst_ref=at, send_sem=c_send.at[0, 0], recv_sem=c_recv.at[g, q],
                     device_id=(sibling, t), device_id_type=MESH,
                 ).wait_recv()
 
-    def use(shard, q, k):
-        c_go(shard, q, k, False)
-        multiply(shard, q, k)
-
-    for tick in range(len(rounds) + n_tensor - 1 - reach):
+    def own_block(q):
+        at = pl.ds(pl.multiple_of(s * part, part), part)
+        cols[q, at, :] = rows[lax.div(s, halves), lax.rem(s, halves), q * part : (q + 1) * part, :]
+
+    ticks = len(rounds) + n_tensor - 1 - reach
+    for tick in range(ticks):
         if tick > 0 and tick + AHEAD < len(rounds):
             send_own(tick + AHEAD)
-        for d in range(1, n_tensor):
+        taken = []
+        for d in range(n_tensor - 1, 0, -1):
             p = tick - max(0, d - reach)
-            if not 0 <= p < len(rounds):
-                continue
-            q, k = rounds[p]
-
+            if 0 <= p < len(rounds):
+                taken.append((d, *rounds[p]))
+        for d, q, k in taken:
             @pl.when(t >= d)
             def _():
                 z_copy(t - d, q, k, 1, False).wait_recv()
                 if d >= reach:
                     z_go(t - d, q, k, 0, False)
-                use(t - d, q, k)
+                c_go(t - d, q, k, False)
 
             @pl.when(t + d < n_tensor)
             def _():
                 z_copy(t + d, q, k, 0, False).wait_recv()
                 if d >= reach:
                     z_go(t + d, q, k, 1, False)
-                use(t + d, q, k)
+                c_go(t + d, q, k, False)
+
+        if tick == 0:
+            for copy in first_copies:
+                copy.wait()
+        for e in range(experts):
+            if tick == 0:
+                prepare(e)
+        if tick == 0:
+            for i in range(1, n_seq // 2):
+                w_copy(i).start()
+            w_copy(0).start()
+        if tick == 0:
+            for copy in own_copies:
+                copy.wait()
+            weight_copy.wait()
+            raw[...] = jnp.zeros_like(raw)
+        for d, q, k in taken:
+            @pl.when(t >= d)
+            def _():
+                multiply(t - d, q, k)
+
+            @pl.when(t + d < n_tensor)
+            def _():
+                multiply(t + d, q, k)
 
         if tick < len(rounds):
             multiply(t, *rounds[tick])
-        if tick == min(1, len(rounds) - 1):
+        if tick == min(2, ticks - 1):
             for i in range(1, n_seq // 2):
                 f_copy(i).wait_recv()
                 f_copy(i).start()
-
-    cols[pl.ds(pl.multiple_of(s * tokens, tokens), tokens), :] = rows[lax.div(s, halves), lax.rem(s, halves)]
+        if tick == ticks - EARLY:
+            wait_weighted()
+            for q in range(PIECES - 1):
+                wait_groups(q)
+                own_block(q)
+                add_groups(q)
+
+    own_block(PIECES - 1)
     for e in range(experts):
         hot, live = token_slots(tok_ref, count_ref, e, tokens)
         part_raw = raw[:, e * hidden : (e + 1) * hidden]
@@ -243,19 +283,8 @@
         )
         prob_out[0, e : e + 1, :] = jnp.sum(jnp.where(live, sums, 0.0), axis=0, keepdims=True)
 
-    for g in range(n_seq):
-        @pl.when(lax.rem(g, 2) != lax.rem(s, 2))
-        def _():
-            at = scaled.at[pl.ds(g * tokens, tokens), :]
-            pltpu.make_async_remote_copy(
-                src_ref=at, dst_ref=at, send_sem=w_send.at[0], recv_sem=w_recv.at[g],
-                device_id=(sibling, t), device_id_type=MESH,
-            ).wait_recv()
-    for q in range(PIECES):
-        wait_groups(q)
-        add_groups(q, q == 0)
-    for e in range(experts):
-        weight_out[e] = total[e * hidden : (e + 1) * hidden, :].astype(jnp.bfloat16)
+    wait_groups(PIECES - 1)
+    add_groups(PIECES - 1)
 
     for i in range(n_seq // 2):
         w_copy(i).wait_send()
@@ -310,14 +339,14 @@
             pltpu.VMEM((experts, tokens), jnp.int32),
             pltpu.VMEM((experts, tokens), jnp.float32),
             pltpu.VMEM((n_tensor, halves, tokens, block), jnp.bfloat16),
-            pltpu.VMEM((n_seq * tokens, block), jnp.bfloat16),
-            pltpu.VMEM((n_seq * tokens, experts * hidden), jnp.bfloat16),
+            pltpu.VMEM((PIECES, n_seq * tokens // PIECES, block), jnp.bfloat16),
+            pltpu.VMEM((PIECES, n_seq * tokens // PIECES, experts * hidden), jnp.bfloat16),
             pltpu.VMEM((experts, hidden, width), jnp.bfloat16),
             pltpu.VMEM((experts, tokens, 2 * hidden), jnp.bfloat16),
             pltpu.VMEM((experts, tokens, 2 * hidden), jnp.float32),
             pltpu.VMEM((tokens, experts * hidden), jnp.bfloat16),
             pltpu.VMEM((tokens, experts * hidden), jnp.float32),
-            pltpu.VMEM((experts * hidden, block), jnp.float32),
+            pltpu.VMEM((experts, hidden, block), jnp.float32),
             dma((5 + halves,)),
             dma((2, reach, pieces)),
             dma((2, n_tensor, pieces)),

time: 35.8 us -> 32.5 us (0.908); the launches traced: 35.1 us -> 32.4 us
  Pallas kernels: 32.4 us -> 29.7 us
    pallas_call x1, Pallas kernels: 32.4 us -> 29.7 us  [per_device(): pl.pallas_call(functools.partial(kernel, n_seq, n_tensor), out_shape=(jax...]
where the time goes in v3:
time: 32.5 us; the launch traced here: 32.4 us
  Pallas kernels  29.7 us (91%)
  local copies, waits for them, and re-layouts  2.06 us (6%)
  between operations  0.64 us (2%)
    pallas_call x1, Pallas kernels, per_device(): pl.pallas_call(functools.partial(kernel, n_seq, n_tensor), out_shape=(jax...  29.7 us
    unnamed x3, local copies, waits for them, and re-layouts  2.06 us

profile of v3, /device:TPU:7, one launch (start us, length us, event | category | flops | bytes accessed | tf_op | source)
XLA Modules:
  0.0 32.4 jit_solution(4857403280812169769)
XLA Ops:
  0.6 29.7 %shard_map.85 = (bf16[1,2,128,512]{3,2,1,0:T(8,128)(2,1)S(1)}, f32[1,2,128]{2,1,0:T(2,128)S(1)}, bf16[2,256,512]{2,1,0:T(8,128)(2,1)S(1)}) custom-call(s32[1,2]{1,0:T(1,128)} %count_in.1, s32[1,2,128]{2,1,0:T(2,128)} %tok_in.1, f32[1,2,128]{2,1,0:T(2,128)} %prob_in.1, bf16[128,1024]{1,0:T(8,128)(2,1)} %grad_ref.1, bf16[2,256,4096]{2,1,0:T(8,128)(2,1)} %weight_ref.1, ...), custom_call_target="tpu_custom_call" | custom-call | tf_op jit(solution)/shard_map/pallas_call | solution.py:328
  30.3 0.7 %copy.12 = bf16[1,2,128,512]{3,2,1,0:T(8,128)(2,1)} copy(bf16[1,2,128,512]{3,2,1,0:T(8,128)(2,1)S(1)} %get-tuple-element.6) | data formatting | bytes 524288
  31.0 0.6 %copy.13 = f32[1,2,128]{2,1,0:T(2,128)} copy(f32[1,2,128]{2,1,0:T(2,128)S(1)} %get-tuple-element.7) | data formatting | bytes 2048
  31.6 0.8 %copy.14 = bf16[2,256,512]{2,1,0:T(8,128)(2,1)} copy(bf16[2,256,512]{2,1,0:T(8,128)(2,1)S(1)} %get-tuple-element.8) | data formatting | bytes 1048576

commit v4 on v3

--- a/solution.py
+++ b/solution.py
@@ -211,26 +211,6 @@
     for tick in range(ticks):
         if tick > 0 and tick + AHEAD < len(rounds):
             send_own(tick + AHEAD)
-        taken = []
-        for d in range(n_tensor - 1, 0, -1):
-            p = tick - max(0, d - reach)
-            if 0 <= p < len(rounds):
-                taken.append((d, *rounds[p]))
-        for d, q, k in taken:
-            @pl.when(t >= d)
-            def _():
-                z_copy(t - d, q, k, 1, False).wait_recv()
-                if d >= reach:
-                    z_go(t - d, q, k, 0, False)
-                c_go(t - d, q, k, False)
-
-            @pl.when(t + d < n_tensor)
-            def _():
-                z_copy(t + d, q, k, 0, False).wait_recv()
-                if d >= reach:
-                    z_go(t + d, q, k, 1, False)
-                c_go(t + d, q, k, False)
-
         if tick == 0:
             for copy in first_copies:
                 copy.wait()
@@ -241,6 +221,26 @@
             for i in range(1, n_seq // 2):
                 w_copy(i).start()
             w_copy(0).start()
+        taken = []
+        for d in range(n_tensor - 1, 0, -1):
+            p = tick - max(0, d - reach)
+            if 0 <= p < len(rounds):
+                taken.append((d, *rounds[p]))
+        for d, q, k in taken:
+            @pl.when(t >= d)
+            def _():
+                z_copy(t - d, q, k, 1, False).wait_recv()
+                if d >= reach:
+                    z_go(t - d, q, k, 0, False)
+                c_go(t - d, q, k, False)
+
+            @pl.when(t + d < n_tensor)
+            def _():
+                z_copy(t + d, q, k, 0, False).wait_recv()
+                if d >= reach:
+                    z_go(t + d, q, k, 1, False)
+                c_go(t + d, q, k, False)
+
         if tick == 0:
             for copy in own_copies:
                 copy.wait()

time: 32.5 us -> 33.2 us (1.022)
  Pallas kernels: 29.7 us -> 30.4 us
    pallas_call x1, Pallas kernels: 29.7 us -> 30.4 us  [per_device(): pl.pallas_call(functools.partial(kernel, n_seq, n_tensor), out_shape=(jax...]
where the time goes in v4:
time: 33.2 us; the launch traced here: 33.1 us
  Pallas kernels  30.4 us (92%)
  local copies, waits for them, and re-layouts  2.06 us (6%)
  between operations  0.64 us (2%)
    pallas_call x1, Pallas kernels, per_device(): pl.pallas_call(functools.partial(kernel, n_seq, n_tensor), out_shape=(jax...  30.4 us
    unnamed x3, local copies, waits for them, and re-layouts  2.06 us

profile of v4, /device:TPU:7, one launch (start us, length us, event | category | flops | bytes accessed | tf_op | source)
XLA Modules:
  0.0 33.1 jit_solution(10751373074385591370)
XLA Ops:
  0.6 30.4 %shard_map.85 = (bf16[1,2,128,512]{3,2,1,0:T(8,128)(2,1)S(1)}, f32[1,2,128]{2,1,0:T(2,128)S(1)}, bf16[2,256,512]{2,1,0:T(8,128)(2,1)S(1)}) custom-call(s32[1,2]{1,0:T(1,128)} %count_in.1, s32[1,2,128]{2,1,0:T(2,128)} %tok_in.1, f32[1,2,128]{2,1,0:T(2,128)} %prob_in.1, bf16[128,1024]{1,0:T(8,128)(2,1)} %grad_ref.1, bf16[2,256,4096]{2,1,0:T(8,128)(2,1)} %weight_ref.1, ...), custom_call_target="tpu_custom_call" | custom-call | tf_op jit(solution)/shard_map/pallas_call | solution.py:328
  31.0 0.7 %copy.12 = bf16[1,2,128,512]{3,2,1,0:T(8,128)(2,1)} copy(bf16[1,2,128,512]{3,2,1,0:T(8,128)(2,1)S(1)} %get-tuple-element.6) | data formatting | bytes 524288
  31.7 0.6 %copy.13 = f32[1,2,128]{2,1,0:T(2,128)} copy(f32[1,2,128]{2,1,0:T(2,128)S(1)} %get-tuple-element.7) | data formatting | bytes 2048
  32.3 0.8 %copy.14 = bf16[2,256,512]{2,1,0:T(8,128)(2,1)} copy(bf16[2,256,512]{2,1,0:T(8,128)(2,1)S(1)} %get-tuple-element.8) | data formatting | bytes 1048576
